TPU v7x, 32 devices: a whole 2x2x4 slice. The times are simulated.
32 devices in a mesh: dp: 8 (over z, core), expert: 4 (over y, x).
Axes of the slice: x: 2, y: 2, z: 4, core: 2. Of those that a mesh axis runs over, the one named last changes fastest.
Arguments:
- tokens: bfloat16 [4, 1024, 3584], P('expert', 'dp'), may hold values from -6 to 6
- grad_out: bfloat16 [4, 1024, 3584], P('expert', 'dp'), may hold values from -6 to 6
- route_ids: int32 [4, 1024], P('expert', 'dp'), may hold values from 0 to 3, as said below
- route_gates: float32 [4, 1024], P('expert', 'dp'), may hold values from 0.2 to 1
- w_gate: bfloat16 [4, 3584, 1024], P('expert', 'dp'), may hold values from -0.09375 to 0.09375
- w_up: bfloat16 [4, 3584, 1024], P('expert', 'dp'), may hold values from -0.09375 to 0.09375
- w_down: bfloat16 [4, 1024, 3584], P('expert', 'dp'), may hold values from -0.1875 to 0.1875
Outputs:
- moe_out: bfloat16 [4, 1024, 3584], P('expert', 'dp')
- input_grad: bfloat16 [4, 1024, 3584], P('expert', None, 'dp')
- gate_grad: float32 [4, 1024], P('expert', 'dp')
Inputs may be any that keep to these rules, and one draw needn't show every extreme that they name: `route_ids`: among the 128 tokens of one device at most 80 name the same expert; one expert is named by exactly 80 tokens of every device; on one device the counts of the other experts differ by at most one.
All inputs are finite; a program needn't handle non-finite values.
Results may differ from a plain program's by a relative error of at most 0.0057.
Values may be sent and summed in bfloat16 or wider, within the bound.
A program may use at most 128 MiB of HBM per device.

v0:
```python
import jax
import jax.numpy as jnp
from jax import lax
from jax.sharding import PartitionSpec as P


def slot_table(route_line, expert_count, capacity):
    chosen = (route_line[:, None] == jnp.arange(expert_count, dtype=jnp.int32)[None, :]).astype(
        jnp.int32
    )
    placed = jnp.sum((jnp.cumsum(chosen, axis=0) - 1) * chosen, axis=1)
    return route_line * capacity + placed


def local(tokens, grad_out, route_ids, route_gates, w_gate, w_up, w_down):
    expert_count = lax.axis_size("expert")
    tok_count = tokens.shape[1]
    width = tokens.shape[2]
    capacity = max(2, 5 * tok_count // (2 * expert_count))
    own_ids = route_ids[0]
    own_slots = slot_table(own_ids, expert_count, capacity)
    slot_owner = jnp.full((expert_count * capacity,), tok_count, jnp.int32)
    slot_owner = slot_owner.at[own_slots].set(jnp.arange(tok_count, dtype=jnp.int32))
    own_tokens = tokens[0]
    own_grad = grad_out[0]
    gate_column = route_gates[0][:, None]
    scaled_grad = (gate_column * own_grad.astype(jnp.float32)).astype(jnp.bfloat16)
    zero_row = jnp.zeros((1, width), jnp.bfloat16)
    send_tokens = jnp.concatenate([own_tokens, zero_row])[slot_owner].reshape(
        expert_count, capacity, width
    )
    send_grad = jnp.concatenate([scaled_grad, zero_row])[slot_owner].reshape(
        expert_count, capacity, width
    )
    arrived_tokens = lax.all_to_all(send_tokens, "expert", split_axis=0, concat_axis=0, tiled=True)
    routed = arrived_tokens.reshape(expert_count * capacity, width)
    full_gate, full_up, full_down = (
        lax.all_gather(w_gate, "dp", axis=1, tiled=True),
        lax.all_gather(w_up, "dp", axis=1, tiled=True),
        lax.all_gather(w_down, "dp", axis=1, tiled=True),
    )
    gate_matrix = full_gate[0]
    up_matrix = full_up[0]
    down_matrix = full_down[0]
    gate_pre = jnp.dot(routed, gate_matrix, preferred_element_type=jnp.float32)
    up_pre = jnp.dot(routed, up_matrix, preferred_element_type=jnp.float32)
    sigmoid_gate = jax.nn.sigmoid(gate_pre)
    silu_gate = gate_pre * sigmoid_gate
    hidden = (silu_gate * up_pre).astype(jnp.bfloat16)
    expert_out = jnp.dot(hidden, down_matrix, preferred_element_type=jnp.float32).astype(
        jnp.bfloat16
    )
    returned = lax.all_to_all(
        expert_out.reshape(expert_count, capacity, width),
        "expert",
        split_axis=0,
        concat_axis=0,
        tiled=True,
    )
    token_out = returned.reshape(expert_count * capacity, width)[own_slots]
    moe_out = (gate_column * token_out.astype(jnp.float32)).astype(jnp.bfloat16)
    gate_grad = jnp.sum(own_grad.astype(jnp.float32) * token_out.astype(jnp.float32), axis=1)
    arrived_grad = lax.all_to_all(send_grad, "expert", split_axis=0, concat_axis=0, tiled=True)
    routed_grad = arrived_grad.reshape(expert_count * capacity, width)
    hidden_grad = jnp.dot(routed_grad, down_matrix.T, preferred_element_type=jnp.float32)
    gate_pre_grad = (
        hidden_grad * up_pre * sigmoid_gate * (1.0 + gate_pre * (1.0 - sigmoid_gate))
    ).astype(jnp.bfloat16)
    up_pre_grad = (hidden_grad * silu_gate).astype(jnp.bfloat16)
    total = jnp.dot(gate_pre_grad, gate_matrix.T, preferred_element_type=jnp.float32)
    input_rows = (
        total + jnp.dot(up_pre_grad, up_matrix.T, preferred_element_type=jnp.float32)
    ).astype(jnp.bfloat16)
    home_rows = lax.all_to_all(
        input_rows.reshape(expert_count, capacity, width),
        "expert",
        split_axis=0,
        concat_axis=0,
        tiled=True,
    )
    token_grad = home_rows.reshape(expert_count * capacity, width)[own_slots]
    input_grad = lax.all_to_all(token_grad[None], "dp", split_axis=2, concat_axis=1, tiled=True)
    return (moe_out[None], input_grad, gate_grad[None])


def solution(mesh):
    in_specs = (
        P("expert", "dp", None),
        P("expert", "dp", None),
        P("expert", "dp"),
        P("expert", "dp"),
        P("expert", "dp", None),
        P("expert", "dp", None),
        P("expert", "dp", None),
    )
    out_specs = (P("expert", "dp", None), P("expert", None, "dp"), P("expert", "dp"))
    return jax.shard_map(local, mesh=mesh, in_specs=in_specs, out_specs=out_specs, check_vma=False)
```

profile of v0, /device:TPU:0, one launch (start us, length us, event | category | flops | bytes accessed | tf_op | source)
XLA Modules:
  0.0 416.3 jit_solution(1568874448295475949)
XLA Ops:
  11.0 3.1 gather_fusion
  14.1 32.7 %all_to_all.38 = bf16[4,80,3584]{2,1,0:T(8,128)(2,1)} all-to-all(bf16[4,80,3584]{2,1,0:T(8,128)(2,1)S(1)} %bitcast.67), channel_id=1, replica_groups=mesh['dp'=8,'expert'=4] {'expert'}, dimensions={0} | all-to-all | bytes 4587520 | tf_op jit(solution)/shard_map/all_to_all | solution.py:35
  46.8 39.0 %all-gather.4.cloned.1.call-done = bf16[1,3584,1024]{2,1,0:T(8,128)(2,1)} async-done(((bf16[1,448,1024]{2,1,0:T(8,128)(2,1)}), bf16[1,3584,1024]{2,1,0:T(8,128)(2,1)}) %all-gather.4.cloned.1.call-update) | async-done | bytes 7340048 | tf_op jit(solution)/shard_map/all_gather | solution.py:38
  85.8 7.5 %fusion.10 = f32[320,1024]{1,0:T(8,128)} fusion(bf16[320,3584]{1,0:T(8,128)(2,1)} %bitcast.72, bf16[1,3584,1024]{2,1,0:T(8,128)(2,1)} %all-gather.4.cloned.1.call-done), kind=kOutput, calls=%fused_computation.15 | convolution fusion | flops 2348810240 | bytes 10944512 | tf_op jit(solution)/shard_map/dot_general | solution.py:45
  93.3 66.2 %all-gather.6.cloned.1.call-done = bf16[1,3584,1024]{2,1,0:T(8,128)(2,1)} async-done(((bf16[1,448,1024]{2,1,0:T(8,128)(2,1)}), bf16[1,3584,1024]{2,1,0:T(8,128)(2,1)}) %all-gather.6.cloned.1.call-update) | async-done | bytes 7340048 | tf_op jit(solution)/shard_map/all_gather | solution.py:39
  159.5 6.8 %fusion.6 = f32[320,1024]{1,0:T(8,128)} fusion(bf16[320,3584]{1,0:T(8,128)(2,1)S(1)} %bitcast.73, bf16[1,3584,1024]{2,1,0:T(8,128)(2,1)} %all-gather.6.cloned.1.call-done), kind=kOutput, calls=%fused_computation.11 | convolution fusion | flops 2348810240 | bytes 10944512 | tf_op jit(solution)/shard_map/dot_general | solution.py:46
  166.2 66.9 %all-gather.8.cloned.1.call-done = bf16[1,1024,3584]{2,1,0:T(8,128)(2,1)} async-done(((bf16[1,128,3584]{2,1,0:T(8,128)(2,1)}), bf16[1,1024,3584]{2,1,0:T(8,128)(2,1)}) %all-gather.8.cloned.1.call-update) | async-done | bytes 7340048 | tf_op jit(solution)/shard_map/all_gather | solution.py:40
  233.1 7.9 %fusion.18 = bf16[320,3584]{1,0:T(8,128)(2,1)} fusion(bf16[1,1024,3584]{2,1,0:T(8,128)(2,1)} %all-gather.8.cloned.1.call-done, f32[320,1024]{1,0:T(8,128)} %fusion.6, f32[320,1024]{1,0:T(8,128)} %fusion.10), kind=kOutput, calls=%fused_computation.19 | convolution fusion | flops 2351923200 | bytes 12255232 | tf_op jit(solution)/shard_map/dot_general | solution.py:50
  241.0 3.7 all-to-all-start.1
  244.7 27.6 %all-to-all-done.1 = bf16[4,80,3584]{2,1,0:T(8,128)(2,1)S(1)} async-done(((bf16[4,80,3584]{2,1,0:T(8,128)(2,1)}), bf16[4,80,3584]{2,1,0:T(8,128)(2,1)S(1)}, u32[]{:S(2)}, u32[]{:S(2)}) %all-to-all-start.1) | async-done | bytes 2293792 | tf_op jit(solution)/shard_map/all_to_all | solution.py:53
  273.4 2.5 fusion.24
  276.0 3.1 gather_fusion.2
  279.1 30.1 %all_to_all.39 = bf16[4,80,3584]{2,1,0:T(8,128)(2,1)S(1)} all-to-all(bf16[4,80,3584]{2,1,0:T(8,128)(2,1)S(1)} %bitcast.66), channel_id=1, replica_groups=mesh['dp'=8,'expert'=4] {'expert'}, dimensions={0} | all-to-all | bytes 4587520 | tf_op jit(solution)/shard_map/all_to_all | solution.py:63
  309.3 5.8 %fusion = f32[320,1024]{1,0:T(8,128)S(1)} fusion(bf16[320,3584]{1,0:T(8,128)(2,1)S(1)} %bitcast.76, bf16[1,1024,3584]{2,1,0:T(8,128)(2,1)} %all-gather.8.cloned.1.call-done), kind=kOutput, calls=%fused_computation.5 | convolution fusion | flops 2348810240 | bytes 10944512 | tf_op jit(solution)/shard_map/dot_general | solution.py:65
  316.2 4.8 %fusion.4 = f32[320,3584]{1,0:T(8,128)} fusion(bf16[1,3584,1024]{2,1,0:T(8,128)(2,1)S(1)} %bitcast.87, f32[320,1024]{1,0:T(8,128)S(1)} %fusion, f32[320,1024]{1,0:T(8,128)S(1)} %copy-done.6), kind=kOutput, calls=%fused_computation.9 | convolution fusion | flops 2350776320 | bytes 14548992 | tf_op jit(solution)/shard_map/dot_general | solution.py:72
  320.9 6.0 %fusion.15 = bf16[320,3584]{1,0:T(8,128)(2,1)S(1)} fusion(f32[320,3584]{1,0:T(8,128)} %fusion.4, bf16[1,3584,1024]{2,1,0:T(8,128)(2,1)S(1)} %bitcast.85, f32[320,1024]{1,0:T(8,128)S(1)} %copy-done.6, f32[320,1024]{1,0:T(8,128)} %copy-done.7, f32[320,1024]{1,0:T(8,128)} %fusion.6), kind=kOutput, calls=%fused_computation.18 | convolution fusion | flops 2354380800 | bytes 18153472 | tf_op jit(solution)/shard_map/dot_general | solution.py:70
  326.9 28.4 %all_to_all.40 = bf16[4,80,3584]{2,1,0:T(8,128)(2,1)S(1)} all-to-all(bf16[4,80,3584]{2,1,0:T(8,128)(2,1)S(1)} %bitcast.75), channel_id=1, replica_groups=mesh['dp'=8,'expert'=4] {'expert'}, dimensions={0} | all-to-all | bytes 4587520 | tf_op jit(solution)/shard_map/all_to_all | solution.py:74
  356.5 2.5 copy.14
  359.5 19.7 %reduce = bf16[3584,128]{1,0:T(8,128)(2,1)S(1)} reduce(bf16[3584,1,128]{2,1,0:T(2,128)(2,1)S(1)} %bitcast.68, bf16[]{:T(256)} %broadcast.103), dimensions={1}, to_apply=%bitcast.58.reduce_sub_computation | reduce | bytes 1835010
  379.2 1.1 reshape.155
  380.3 3.6 all-to-all-start.4
  383.9 1.1 fusion.22
  385.0 22.6 %all-to-all-done.4 = bf16[8,2,28672]{2,1,0:T(2,128)(2,1)S(1)} async-done(((bf16[8,2,28672]{2,1,0:T(2,128)(2,1)}), bf16[8,2,28672]{2,1,0:T(2,128)(2,1)S(1)}, u32[]{:S(2)}, u32[]{:S(2)}) %all-to-all-start.4) | async-done | bytes 917536 | tf_op jit(solution)/shard_map/all_to_all | solution.py:82
  408.6 1.2 copy.19
  (48 shorter events, 8.6 us)
Async XLA Ops:
  7.2 2.2 copy-start.4
  7.2 2.5 copy-start.3
  7.2 78.6 %all-gather.4.cloned.1.call-start = ((), (), s32[]{:S(2)}) async-start(), calls=%async_computation.5 | async-start | bytes 8257536 | tf_op jit(solution)/shard_map/all_gather | solution.py:38
  7.9 151.5 %all-gather.6.cloned.1.call-start = ((), (), s32[]{:S(2)}) async-start(), calls=%async_computation.6 | async-start | bytes 8257536 | tf_op jit(solution)/shard_map/all_gather | solution.py:39
  8.7 224.5 %all-gather.8.cloned.1.call-start = ((), (), s32[]{:S(2)}) async-start(), calls=%async_computation.7 | async-start | bytes 8257536 | tf_op jit(solution)/shard_map/all_gather | solution.py:40
  85.8 73.7 %copy-start.2 = (bf16[4,80,3584]{2,1,0:T(8,128)(2,1)S(1)}, bf16[4,80,3584]{2,1,0:T(8,128)(2,1)}, u32[]{:S(2)}) copy-start(bf16[4,80,3584]{2,1,0:T(8,128)(2,1)} %all_to_all.38) | copy-start | bytes 6881284
  241.0 31.3 %all-to-all-start.1 = ((bf16[4,80,3584]{2,1,0:T(8,128)(2,1)}), bf16[4,80,3584]{2,1,0:T(8,128)(2,1)S(1)}, u32[]{:S(2)}, u32[]{:S(2)}) async-start(bf16[4,80,3584]{2,1,0:T(8,128)(2,1)} %bitcast.74), calls=%async_computation.1 | async-start | bytes 4587520 | tf_op jit(solution)/shard_map/all_to_all | solution.py:53
  272.3 1.1 copy-start.5
  273.4 2.5 copy-start
  279.1 37.1 %slice-start.2 = ((s8[7340032]{0:T(1024)(128)(4,1)}), s8[4194304]{0:T(1024)(128)(4,1)S(1)}, s32[]{:S(2)}) async-start(s8[7340032]{0:T(1024)(128)(4,1)} %bitcast.86), calls=%async_computation.10 | async-start | bytes 8388608
  309.3 6.9 %slice-start.3 = ((s8[7340032]{0:T(1024)(128)(4,1)}), s8[3145728]{0:T(1024)(128)(4,1)S(1)}, s32[]{:S(2)}) async-start(s8[7340032]{0:T(1024)(128)(4,1)} %bitcast.86), calls=%async_computation.11 | async-start | bytes 6291456
  309.3 6.9 %copy-start.6 = (f32[320,1024]{1,0:T(8,128)S(1)}, f32[320,1024]{1,0:T(8,128)}, u32[]{:S(2)}) copy-start(f32[320,1024]{1,0:T(8,128)} %fusion.10) | copy-start | bytes 3932164
  309.3 11.7 %slice-start = ((s8[7340032]{0:T(1024)(128)(4,1)}), s8[4194304]{0:T(1024)(128)(4,1)S(1)}, s32[]{:S(2)}) async-start(s8[7340032]{0:T(1024)(128)(4,1)} %bitcast.84), calls=%async_computation.8 | async-start | bytes 8388608
  315.1 1.1 copy-start.7
  316.2 4.8 %slice-start.1 = ((s8[7340032]{0:T(1024)(128)(4,1)}), s8[3145728]{0:T(1024)(128)(4,1)S(1)}, s32[]{:S(2)}) async-start(s8[7340032]{0:T(1024)(128)(4,1)} %bitcast.84), calls=%async_computation.9 | async-start | bytes 6291456
  379.2 4.7 %copy-start.1 = (bf16[128,3584]{1,0:T(8,128)(2,1)S(1)}, bf16[128,3584]{1,0:T(8,128)(2,1)}, u32[]{:S(2)}) copy-start(bf16[128,3584]{1,0:T(8,128)(2,1)} %copy-done) | copy-start | bytes 2752516
  380.3 27.3 %all-to-all-start.4 = ((bf16[8,2,28672]{2,1,0:T(2,128)(2,1)}), bf16[8,2,28672]{2,1,0:T(2,128)(2,1)S(1)}, u32[]{:S(2)}, u32[]{:S(2)}) async-start(bf16[8,2,28672]{2,1,0:T(2,128)(2,1)} %reshape.155), calls=%async_computation.4 | async-start | bytes 1835008 | tf_op jit(solution)/shard_map/all_to_all | solution.py:82
Sparse Core Ops, SparseCore 0:
  9.7 76.0 all-gather.3
  87.4 71.9 all-gather.5
  161.1 71.9 all-gather.7
where the time goes:
time: 417 us; the launch traced here: 416 us
  waiting for transfers between devices  224 us (54%)
  blocking collectives  91.3 us (22%)
  matrix products  38.7 us (9%)
  other arithmetic  23.7 us (6%)
  local copies, waits for them, and re-layouts  17.1 us (4%)
  between operations  14 us (3%)
  starting transfers between devices  7.35 us (2%)
    all_gather x1, waiting for transfers between devices, local(): lax.all_gather(w_down, 'dp', axis=1, tiled=True)  66.9 us
    all_gather x1, waiting for transfers between devices, local(): lax.all_gather(w_up, 'dp', axis=1, tiled=True)  66.2 us
    all_gather x1, waiting for transfers between devices, local(): lax.all_gather(w_gate, 'dp', axis=1, tiled=True)  39 us
    all_to_all x1, blocking collectives, local(): lax.all_to_all(send_tokens, 'expert', split_axis=0, concat_axis=0, tiled=...  32.7 us
    all_to_all x1, blocking collectives, local(): lax.all_to_all(send_grad, 'expert', split_axis=0, concat_axis=0, tiled=True)  30.1 us
    all_to_all x1, blocking collectives, local(): lax.all_to_all(input_rows.reshape(expert_count, capacity, width), 'expert...  28.4 us
    all_to_all x1, waiting for transfers between devices, local(): lax.all_to_all(expert_out.reshape(expert_count, capacity, width), 'expert...  27.6 us
    all_to_all x1, waiting for transfers between devices, local(): lax.all_to_all(token_grad[None], 'dp', split_axis=2, concat_axis=1, tiled...  22.6 us
  transfers between devices with their start and end apart: 5, of which 5 were waited for; matrix products, arithmetic and copies ran while one was open for 5% of the time, Pallas kernels for 0%

commit v1 on v0

--- a/solution.py
+++ b/solution.py
@@ -2,6 +2,22 @@
 import jax.numpy as jnp
 from jax import lax
 from jax.sharding import PartitionSpec as P
+
+
+def close_panel(q_in):
+    amount_of = lax.axis_size("dp")
+    shelf = [(tick, (tick + 1) % amount_of) for tick in range(amount_of)]
+    log = [(tick, (tick - 1) % amount_of) for tick in range(amount_of)]
+    s_next, val2 = ([q_in], [q_in])
+    for _ in range(amount_of // 2):
+        x_new = lax.ppermute(s_next[-1], "dp", perm=shelf)
+        s_next.append(x_new)
+    for _ in range((amount_of - 1) // 2):
+        all_values = lax.ppermute(val2[-1], "dp", log)
+        val2.append(all_values)
+    x_next = jnp.concatenate([*s_next[::-1], *val2[1:]], axis=1)
+    piece_next = lax.axis_index("dp")
+    return jnp.roll(x_next, shift=(piece_next - amount_of // 2) * q_in.shape[1], axis=1)
 
 
 def slot_table(route_line, expert_count, capacity):
@@ -37,7 +53,7 @@
     full_gate, full_up, full_down = (
         lax.all_gather(w_gate, "dp", axis=1, tiled=True),
         lax.all_gather(w_up, "dp", axis=1, tiled=True),
-        lax.all_gather(w_down, "dp", axis=1, tiled=True),
+        close_panel(w_down),
     )
     gate_matrix = full_gate[0]
     up_matrix = full_up[0]

time: 417 us -> 400 us (0.959)
  blocking collectives: 91.3 us -> 58.6 us
  waiting for transfers between devices: 224 us -> 194 us
  local copies, waits for them, and re-layouts: 17.1 us -> 42 us
  starting transfers between devices: 7.35 us -> 29.5 us
    ppermute x0 -> x7, waiting for transfers between devices: none -> 99.2 us  [the longest x4 98.1 us: close_panel(): x_new = lax.ppermute(s_next[-1], 'dp', perm=shelf)]
    all_gather x1 -> x0, waiting for transfers between devices: 66.9 us -> none  [local(): lax.all_gather(w_down, 'dp', axis=1, tiled=True)]
    all_gather x1, waiting for transfers between devices: 39 us -> 0.01 us  [local(): lax.all_gather(w_gate, 'dp', axis=1, tiled=True)]
    all_to_all x1 -> x0, blocking collectives: 32.7 us -> none  [local(): lax.all_to_all(send_tokens, 'expert', split_axis=0, concat_axis=0, tiled=...]
    all_gather x1, waiting for transfers between devices: 66.2 us -> 43.1 us  [local(): lax.all_gather(w_up, 'dp', axis=1, tiled=True)]
    unnamed x28 -> x49, local copies, waits for them, and re-layouts: 3.81 us -> 26 us
    ppermute x0 -> x7, starting transfers between devices: none -> 13.8 us  [the longest x3 7.01 us: close_panel(): all_values = lax.ppermute(val2[-1], 'dp', log)]
    all_to_all x0 -> x1, starting transfers between devices: none -> 4.59 us  [local(): lax.all_to_all(send_tokens, 'expert', split_axis=0, concat_axis=0, tiled=...]
  transfers between devices with their start and end apart: 5 -> 12, of which waited for: 5 -> 8; matrix products, arithmetic and copies ran while one was open for 5% -> 9% of each run, Pallas kernels for 0% -> 0%
where the time goes in v1:
time: 400 us; the launch traced here: 399 us
  waiting for transfers between devices  194 us (48%)
  blocking collectives  58.6 us (15%)
  local copies, waits for them, and re-layouts  42 us (10%)
  matrix products  36.6 us (9%)
  starting transfers between devices  29.5 us (7%)
  other arithmetic  24.4 us (6%)
  between operations  14.4 us (4%)
    ppermute x4, waiting for transfers between devices, close_panel(): x_new = lax.ppermute(s_next[-1], 'dp', perm=shelf)  98.1 us
    all_gather x1, waiting for transfers between devices, local(): lax.all_gather(w_up, 'dp', axis=1, tiled=True)  43.1 us
    all_to_all x1, blocking collectives, local(): lax.all_to_all(send_grad, 'expert', split_axis=0, concat_axis=0, tiled=True)  30.1 us
    all_to_all x1, blocking collectives, local(): lax.all_to_all(input_rows.reshape(expert_count, capacity, width), 'expert...  28.5 us
    all_to_all x1, waiting for transfers between devices, local(): lax.all_to_all(expert_out.reshape(expert_count, capacity, width), 'expert...  27.5 us
    unnamed x49, local copies, waits for them, and re-layouts  26 us
    all_to_all x1, waiting for transfers between devices, local(): lax.all_to_all(token_grad[None], 'dp', split_axis=2, concat_axis=1, tiled...  22.6 us
    unnamed x3, other arithmetic  19.7 us
  transfers between devices with their start and end apart: 12, of which 8 were waited for; matrix products, arithmetic and copies ran while one was open for 9% of the time, Pallas kernels for 0%

profile of v1, /device:TPU:0, one launch (start us, length us, event | category | flops | bytes accessed | tf_op | source)
XLA Modules:
  0.0 399.3 jit_solution(7506828545641787136)
XLA Ops:
  9.2 15.4 %collective-permute-done = bf16[1,128,3584]{2,1,0:T(8,128)(2,1)S(1)} collective-permute-done((bf16[1,128,3584]{2,1,0:T(8,128)(2,1)}, bf16[1,128,3584]{2,1,0:T(8,128)(2,1)S(1)}, u32[]{:S(2)}, u32[]{:S(2)}) %collective-permute-start) | collective-permute-done | bytes 917536 | tf_op jit(solution)/shard_map/ppermute | solution.py:13
  24.8 3.3 collective-permute-start.4
  28.1 38.9 %collective-permute-done.1 = bf16[1,128,3584]{2,1,0:T(8,128)(2,1)S(1)} collective-permute-done((bf16[1,128,3584]{2,1,0:T(8,128)(2,1)S(1)}, bf16[1,128,3584]{2,1,0:T(8,128)(2,1)S(1)}, u32[]{:S(2)}, u32[]{:S(2)}) %collective-permute-start.1) | collective-permute-done | bytes 917536 | tf_op jit(solution)/shard_map/ppermute | solution.py:13
  68.2 3.6 collective-permute-start.5
  71.9 29.6 %collective-permute-done.2 = bf16[1,128,3584]{2,1,0:T(8,128)(2,1)} collective-permute-done((bf16[1,128,3584]{2,1,0:T(8,128)(2,1)S(1)}, bf16[1,128,3584]{2,1,0:T(8,128)(2,1)}, u32[]{:S(2)}, u32[]{:S(2)}) %collective-permute-start.2) | collective-permute-done | bytes 917536 | tf_op jit(solution)/shard_map/ppermute | solution.py:13
  101.4 6.0 %collective-permute-start.3 = (bf16[1,128,3584]{2,1,0:T(8,128)(2,1)}, bf16[1,128,3584]{2,1,0:T(8,128)(2,1)}, u32[]{:S(2)}, u32[]{:S(2)}) collective-permute-start(bf16[1,128,3584]{2,1,0:T(8,128)(2,1)} %collective-permute-done.2), channel_id=1, source_target_pairs={{0,4},{4,8},{8,12},{12,16},{16,20},{20,24},{24,28},{28,0},{1,5},{5... | collective-permute-start | bytes 2752520 | tf_op jit(solution)/shard_map/ppermute | solution.py:13
  110.9 3.7 gather_fusion
  114.6 4.6 %all-to-all-start = ((bf16[4,80,3584]{2,1,0:T(8,128)(2,1)}), bf16[4,80,3584]{2,1,0:T(8,128)(2,1)}, u32[]{:S(2)}, u32[]{:S(2)}) async-start(bf16[4,80,3584]{2,1,0:T(8,128)(2,1)} %bitcast.6), calls=%async_computation | async-start | bytes 4587520 | tf_op jit(solution)/shard_map/all_to_all | solution.py:51
  119.3 14.1 %collective-permute-done.3 = bf16[1,128,3584]{2,1,0:T(8,128)(2,1)} collective-permute-done((bf16[1,128,3584]{2,1,0:T(8,128)(2,1)}, bf16[1,128,3584]{2,1,0:T(8,128)(2,1)}, u32[]{:S(2)}, u32[]{:S(2)}) %collective-permute-start.3) | collective-permute-done | bytes 917536 | tf_op jit(solution)/shard_map/ppermute | solution.py:13
  156.6 6.3 %fusion.10 = f32[320,1024]{1,0:T(8,128)S(1)} fusion(bf16[320,3584]{1,0:T(8,128)(2,1)} %bitcast.7, bf16[1,3584,1024]{2,1,0:T(8,128)(2,1)} %all-gather.3.cloned.1.call-done), kind=kOutput, calls=%fused_computation.15 | convolution fusion | flops 2348810240 | bytes 10944512 | tf_op jit(solution)/shard_map/dot_general | solution.py:61
  163.0 43.1 %all-gather.5.cloned.1.call-done = bf16[1,3584,1024]{2,1,0:T(8,128)(2,1)} async-done(((bf16[1,448,1024]{2,1,0:T(8,128)(2,1)}), bf16[1,3584,1024]{2,1,0:T(8,128)(2,1)}) %all-gather.5.cloned.1.call-update) | async-done | bytes 7340048 | tf_op jit(solution)/shard_map/all_gather | solution.py:55
  206.0 6.3 %fusion.6 = f32[320,1024]{1,0:T(8,128)S(1)} fusion(bf16[320,3584]{1,0:T(8,128)(2,1)} %bitcast.7, bf16[1,3584,1024]{2,1,0:T(8,128)(2,1)} %all-gather.5.cloned.1.call-done), kind=kOutput, calls=%fused_computation.11 | convolution fusion | flops 2348810240 | bytes 10944512 | tf_op jit(solution)/shard_map/dot_general | solution.py:62
  212.3 7.5 %fusion.20 = bf16[320,3584]{1,0:T(8,128)(2,1)} fusion(bf16[1,2048,3584]{2,1,0:T(8,128)(2,1)} %constant_dynamic-update-slice_fusion, s32[]{:T(128)S(6)} %select_n.32, f32[320,1024]{1,0:T(8,128)S(1)} %fusion.6, f32[320,1024]{1,0:T(8,128)S(1)} %fusion.10), kind=kOutput, calls=%fused_computation.21 | convolution fusion | flops 2351923200 | bytes 12255236 | tf_op jit(solution)/shard_map/dot_general | solution.py:66
  219.9 4.8 %all-to-all-start.1 = ((bf16[4,80,3584]{2,1,0:T(8,128)(2,1)}), bf16[4,80,3584]{2,1,0:T(8,128)(2,1)S(1)}, u32[]{:S(2)}, u32[]{:S(2)}) async-start(bf16[4,80,3584]{2,1,0:T(8,128)(2,1)} %bitcast.71), calls=%async_computation.1 | async-start | bytes 4587520 | tf_op jit(solution)/shard_map/all_to_all | solution.py:69
  224.6 27.5 %all-to-all-done.1 = bf16[4,80,3584]{2,1,0:T(8,128)(2,1)S(1)} async-done(((bf16[4,80,3584]{2,1,0:T(8,128)(2,1)}), bf16[4,80,3584]{2,1,0:T(8,128)(2,1)S(1)}, u32[]{:S(2)}, u32[]{:S(2)}) %all-to-all-start.1) | async-done | bytes 2293792 | tf_op jit(solution)/shard_map/all_to_all | solution.py:69
  255.8 3.1 gather_fusion.2
  258.9 30.1 %all_to_all.38 = bf16[4,80,3584]{2,1,0:T(8,128)(2,1)S(1)} all-to-all(bf16[4,80,3584]{2,1,0:T(8,128)(2,1)S(1)} %bitcast.66), channel_id=1, replica_groups=mesh['dp'=8,'expert'=4] {'expert'}, dimensions={0} | all-to-all | bytes 4587520 | tf_op jit(solution)/shard_map/all_to_all | solution.py:79
  289.0 5.8 %fusion = f32[320,1024]{1,0:T(8,128)S(1)} fusion(bf16[320,3584]{1,0:T(8,128)(2,1)S(1)} %bitcast.73, bf16[1,2048,3584]{2,1,0:T(8,128)(2,1)} %constant_dynamic-update-slice_fusion, s32[]{:T(128)S(6)} %select_n.32), kind=kOutput, calls=%fused_computation.5 | convolution fusion | flops 2348810240 | bytes 10944516 | tf_op jit(solution)/shard_map/dot_general | solution.py:81
  295.9 4.7 %fusion.4 = f32[320,3584]{1,0:T(8,128)} fusion(bf16[1,3584,1024]{2,1,0:T(8,128)(2,1)S(1)} %bitcast.84, f32[320,1024]{1,0:T(8,128)S(1)} %fusion, f32[320,1024]{1,0:T(8,128)S(1)} %copy-done.8), kind=kOutput, calls=%fused_computation.9 | convolution fusion | flops 2350776320 | bytes 14548992 | tf_op jit(solution)/shard_map/dot_general | solution.py:88
  300.7 6.0 %fusion.17 = bf16[320,3584]{1,0:T(8,128)(2,1)S(1)} fusion(f32[320,3584]{1,0:T(8,128)} %fusion.4, bf16[1,3584,1024]{2,1,0:T(8,128)(2,1)S(1)} %bitcast.82, f32[320,1024]{1,0:T(8,128)S(1)} %copy-done.8, f32[320,1024]{1,0:T(8,128)} %copy-done.10, f32[320,1024]{1,0:T(8,128)} %copy-done.9), kind=kOutput, calls=%fused_computation.20 | convolution fusion | flops 2354380800 | bytes 18153472 | tf_op jit(solution)/shard_map/dot_general | solution.py:86
  306.6 28.5 %all_to_all.39 = bf16[4,80,3584]{2,1,0:T(8,128)(2,1)S(1)} all-to-all(bf16[4,80,3584]{2,1,0:T(8,128)(2,1)S(1)} %bitcast.72), channel_id=1, replica_groups=mesh['dp'=8,'expert'=4] {'expert'}, dimensions={0} | all-to-all | bytes 4587520 | tf_op jit(solution)/shard_map/all_to_all | solution.py:90
  339.3 19.7 %reduce = bf16[3584,128]{1,0:T(8,128)(2,1)S(1)} reduce(bf16[3584,1,128]{2,1,0:T(2,128)(2,1)S(1)} %bitcast.67, bf16[]{:T(256)} %broadcast.104), dimensions={1}, to_apply=%bitcast.58.reduce_sub_computation | reduce | bytes 1835010
  360.1 6.4 %all-to-all-start.4 = ((bf16[8,2,28672]{2,1,0:T(2,128)(2,1)}), bf16[8,2,28672]{2,1,0:T(2,128)(2,1)S(1)}, u32[]{:S(2)}, u32[]{:S(2)}) async-start(bf16[8,2,28672]{2,1,0:T(2,128)(2,1)} %reshape.155), calls=%async_computation.4 | async-start | bytes 1835008 | tf_op jit(solution)/shard_map/all_to_all | solution.py:98
  367.6 22.6 %all-to-all-done.4 = bf16[8,2,28672]{2,1,0:T(2,128)(2,1)S(1)} async-done(((bf16[8,2,28672]{2,1,0:T(2,128)(2,1)}), bf16[8,2,28672]{2,1,0:T(2,128)(2,1)S(1)}, u32[]{:S(2)}, u32[]{:S(2)}) %all-to-all-start.4) | async-done | bytes 917536 | tf_op jit(solution)/shard_map/all_to_all | solution.py:98
  (82 shorter events, 43.3 us)
Async XLA Ops:
  7.2 102.5 %copy-start.5 = (s32[1,128]{1,0:T(1,128)S(1)}, s32[1,128]{1,0:T(1,128)}, u32[]{:S(2)}) copy-start(s32[1,128]{1,0:T(1,128)} %param.9) | copy-start | bytes 1540
  7.2 149.4 %all-gather.3.cloned.1.call-start = ((), (), s32[]{:S(2)}) async-start(), calls=%async_computation.5 | async-start | bytes 8257536 | tf_op jit(solution)/shard_map/all_gather | solution.py:54
  7.9 198.1 %all-gather.5.cloned.1.call-start = ((), (), s32[]{:S(2)}) async-start(), calls=%async_computation.6 | async-start | bytes 8257536 | tf_op jit(solution)/shard_map/all_gather | solution.py:55
  8.7 15.9 %collective-permute-start = (bf16[1,128,3584]{2,1,0:T(8,128)(2,1)}, bf16[1,128,3584]{2,1,0:T(8,128)(2,1)S(1)}, u32[]{:S(2)}, u32[]{:S(2)}) collective-permute-start(bf16[1,128,3584]{2,1,0:T(8,128)(2,1)} %param.13), channel_id=1, source_target_pairs={{0,4},{4,8},{8,12},{12,16},{16,20},{20,24},{24,28},{28,0},{1,5},{5... | collective-permute-start | bytes 2752520 | tf_op jit(solution)/shard_map/ppermute | solution.py:13
  24.6 42.5 %collective-permute-start.1 = (bf16[1,128,3584]{2,1,0:T(8,128)(2,1)S(1)}, bf16[1,128,3584]{2,1,0:T(8,128)(2,1)S(1)}, u32[]{:S(2)}, u32[]{:S(2)}) collective-permute-start(bf16[1,128,3584]{2,1,0:T(8,128)(2,1)S(1)} %collective-permute-done), channel_id=1, source_target_pairs={{0,4},{4,8},{8,12},{12,16},{16,20},{20,24},{24,28},{28,0},{1,5},{5... | collective-permute-start | bytes 2752520 | tf_op jit(solution)/shard_map/ppermute | solution.py:13
  24.8 43.4 %collective-permute-start.4 = (bf16[1,128,3584]{2,1,0:T(8,128)(2,1)}, bf16[1,128,3584]{2,1,0:T(8,128)(2,1)S(1)}, u32[]{:S(2)}, u32[]{:S(2)}) collective-permute-start(bf16[1,128,3584]{2,1,0:T(8,128)(2,1)} %param.13), channel_id=1, source_target_pairs={{0,28},{4,0},{8,4},{12,8},{16,12},{20,16},{24,20},{28,24},{1,29},{... | collective-permute-start | bytes 2752520 | tf_op jit(solution)/shard_map/ppermute | solution.py:16
  67.1 34.4 %collective-permute-start.2 = (bf16[1,128,3584]{2,1,0:T(8,128)(2,1)S(1)}, bf16[1,128,3584]{2,1,0:T(8,128)(2,1)}, u32[]{:S(2)}, u32[]{:S(2)}) collective-permute-start(bf16[1,128,3584]{2,1,0:T(8,128)(2,1)S(1)} %collective-permute-done.1), channel_id=1, source_target_pairs={{0,4},{4,8},{8,12},{12,16},{16,20},{20,24},{24,28},{28,0},{1,5},{5... | collective-permute-start | bytes 2752520 | tf_op jit(solution)/shard_map/ppermute | solution.py:13
  68.2 51.0 %collective-permute-start.5 = (bf16[1,128,3584]{2,1,0:T(8,128)(2,1)S(1)}, bf16[1,128,3584]{2,1,0:T(8,128)(2,1)}, u32[]{:S(2)}, u32[]{:S(2)}) collective-permute-start(bf16[1,128,3584]{2,1,0:T(8,128)(2,1)S(1)} %collective-permute-done.4), channel_id=1, source_target_pairs={{0,28},{4,0},{8,4},{12,8},{16,12},{20,16},{24,20},{28,24},{1,29},{... | collective-permute-start | bytes 2752520 | tf_op jit(solution)/shard_map/ppermute | solution.py:16
  101.4 32.0 %collective-permute-start.3 = (bf16[1,128,3584]{2,1,0:T(8,128)(2,1)}, bf16[1,128,3584]{2,1,0:T(8,128)(2,1)}, u32[]{:S(2)}, u32[]{:S(2)}) collective-permute-start(bf16[1,128,3584]{2,1,0:T(8,128)(2,1)} %collective-permute-done.2), channel_id=1, source_target_pairs={{0,4},{4,8},{8,12},{12,16},{16,20},{20,24},{24,28},{28,0},{1,5},{5... | collective-permute-start | bytes 2752520 | tf_op jit(solution)/shard_map/ppermute | solution.py:13
  114.6 42.1 %all-to-all-start = ((bf16[4,80,3584]{2,1,0:T(8,128)(2,1)}), bf16[4,80,3584]{2,1,0:T(8,128)(2,1)}, u32[]{:S(2)}, u32[]{:S(2)}) async-start(bf16[4,80,3584]{2,1,0:T(8,128)(2,1)} %bitcast.6), calls=%async_computation | async-start | bytes 4587520 | tf_op jit(solution)/shard_map/all_to_all | solution.py:51
  119.2 18.6 %copy-start.4 = (bf16[1,128,3584]{2,1,0:T(8,128)(2,1)S(1)}, bf16[1,128,3584]{2,1,0:T(8,128)(2,1)}, u32[]{:S(2)}) copy-start(bf16[1,128,3584]{2,1,0:T(8,128)(2,1)} %copy-done.3) | copy-start | bytes 2752516
  119.2 24.8 %collective-permute-start.6 = (bf16[1,128,3584]{2,1,0:T(8,128)(2,1)}, bf16[1,128,3584]{2,1,0:T(8,128)(2,1)S(1)}, u32[]{:S(2)}, u32[]{:S(2)}) collective-permute-start(bf16[1,128,3584]{2,1,0:T(8,128)(2,1)} %collective-permute-done.5), channel_id=1, source_target_pairs={{0,28},{4,0},{8,4},{12,8},{16,12},{20,16},{24,20},{28,24},{1,29},{... | collective-permute-start | bytes 2752520 | tf_op jit(solution)/shard_map/ppermute | solution.py:16
  137.8 2.0 copy-start.2
  162.9 49.4 %copy-start.7 = (f32[320,1024]{1,0:T(8,128)}, f32[320,1024]{1,0:T(8,128)S(1)}, u32[]{:S(2)}) copy-start(f32[320,1024]{1,0:T(8,128)S(1)} %fusion.10) | copy-start | bytes 3932164
  212.3 7.5 %copy-start.9 = (f32[320,1024]{1,0:T(8,128)}, f32[320,1024]{1,0:T(8,128)S(1)}, u32[]{:S(2)}) copy-start(f32[320,1024]{1,0:T(8,128)S(1)} %fusion.6) | copy-start | bytes 3932164
  219.9 32.2 %all-to-all-start.1 = ((bf16[4,80,3584]{2,1,0:T(8,128)(2,1)}), bf16[4,80,3584]{2,1,0:T(8,128)(2,1)S(1)}, u32[]{:S(2)}, u32[]{:S(2)}) async-start(bf16[4,80,3584]{2,1,0:T(8,128)(2,1)} %bitcast.71), calls=%async_computation.1 | async-start | bytes 4587520 | tf_op jit(solution)/shard_map/all_to_all | solution.py:69
  253.2 2.5 copy-start
  258.9 37.0 %slice-start.2 = ((s8[7340032]{0:T(1024)(128)(4,1)}), s8[4194304]{0:T(1024)(128)(4,1)S(1)}, s32[]{:S(2)}) async-start(s8[7340032]{0:T(1024)(128)(4,1)} %bitcast.83), calls=%async_computation.9 | async-start | bytes 8388608
  289.0 6.9 %slice-start.3 = ((s8[7340032]{0:T(1024)(128)(4,1)}), s8[3145728]{0:T(1024)(128)(4,1)S(1)}, s32[]{:S(2)}) async-start(s8[7340032]{0:T(1024)(128)(4,1)} %bitcast.83), calls=%async_computation.10 | async-start | bytes 6291456
  289.0 6.9 %copy-start.8 = (f32[320,1024]{1,0:T(8,128)S(1)}, f32[320,1024]{1,0:T(8,128)}, u32[]{:S(2)}) copy-start(f32[320,1024]{1,0:T(8,128)} %copy-done.7) | copy-start | bytes 3932164
  289.0 11.6 %slice-start = ((s8[7340032]{0:T(1024)(128)(4,1)}), s8[4194304]{0:T(1024)(128)(4,1)S(1)}, s32[]{:S(2)}) async-start(s8[7340032]{0:T(1024)(128)(4,1)} %bitcast.81), calls=%async_computation.7 | async-start | bytes 8388608
  295.9 4.7 %slice-start.1 = ((s8[7340032]{0:T(1024)(128)(4,1)}), s8[3145728]{0:T(1024)(128)(4,1)S(1)}, s32[]{:S(2)}) async-start(s8[7340032]{0:T(1024)(128)(4,1)} %bitcast.81), calls=%async_computation.8 | async-start | bytes 6291456
  359.0 7.5 %copy-start.1 = (bf16[128,3584]{1,0:T(8,128)(2,1)S(1)}, bf16[128,3584]{1,0:T(8,128)(2,1)}, u32[]{:S(2)}) copy-start(bf16[128,3584]{1,0:T(8,128)(2,1)} %copy-done) | copy-start | bytes 2752516
  360.1 30.1 %all-to-all-start.4 = ((bf16[8,2,28672]{2,1,0:T(2,128)(2,1)}), bf16[8,2,28672]{2,1,0:T(2,128)(2,1)S(1)}, u32[]{:S(2)}, u32[]{:S(2)}) async-start(bf16[8,2,28672]{2,1,0:T(2,128)(2,1)} %reshape.155), calls=%async_computation.4 | async-start | bytes 1835008 | tf_op jit(solution)/shard_map/all_to_all | solution.py:98
  (3 other events, 3.3 us)
Sparse Core Ops, SparseCore 0:
  9.7 117.6 all-gather.2
  129.0 77.0 all-gather.4
